TPU v7x, 32 devices: a whole 2x2x4 slice. The times are simulated.
32 devices in a mesh: grid: 16 (over z, x, core), orb: 2 (over y).
Axes of the slice: x: 2, y: 2, z: 4, core: 2. Of those that a mesh axis runs over, the one named last changes fastest.
Arguments:
- orbitals: bfloat16 [1024, 8, 64, 128], P('orb', None, 'grid'), may hold values from -0.0234375 to 0.0234375
- rotated_adj: bfloat16 [128, 8, 64, 128], P(None, None, 'grid'), may hold values from -6 to 6
- level_adj: float32 [128], replicated, may hold values from -240 to 240
- rotation: bfloat16 [1024, 1024], replicated, may hold values from -0.1875 to 0.1875
- gap_inverse: float32 [1024, 1024], P('orb'), may hold values from -10 to 10, as said below
- potential: float32 [8, 64, 128], P(None, 'grid'), may hold values from -4 to 2
- window_cols: int32 [128], replicated, may hold values from 0 to 1023, as said below
- tile_map: int32 [8], replicated, may hold values from 0 to 7, each once
Outputs:
- orbital_adj: bfloat16 [1024, 8, 64, 128], P('orb', None, 'grid')
Inputs may be any that keep to these rules, and one draw needn't show every extreme that they name: `gap_inverse`: entry (i, j) is (l_j - l_i) / ((l_j - l_i) squared + 0.0025) for some real levels l, held within the range. `window_cols`: 128 distinct column indices, among them 0 and 1023. `tile_map`: each tile number once.
All inputs are finite; a program needn't handle non-finite values.
Results may differ from a plain program's by a relative error of at most 0.0069.
Values may be sent and summed in bfloat16 or wider, within the bound.
A program may use at most 192 MiB of HBM per device.

v0:
```python
import jax
import jax.numpy as jnp
from jax import lax
from jax.sharding import PartitionSpec as P


def padded_2(shard, sides, width):
    for axis, dim in sides:
        size, length = (lax.axis_size(axis), shard.shape[dim])
        up = [(i, (i + 1) % size) for i in range(size)]
        down = [(j, i) for i, j in up]
        last = lax.slice_in_dim(shard, length - width, length, axis=dim)
        leading = lax.slice_in_dim(shard, 0, width, axis=dim)
        before = lax.ppermute(last, axis, up)
        after = lax.ppermute(leading, axis, down)
        shard = jnp.concatenate([before, shard, after], axis=dim)
    return shard


def second_diff(field, along):
    nearest = jnp.roll(field, 1, along) + jnp.roll(field, -1, along)
    farther = jnp.roll(field, 2, along) + jnp.roll(field, -2, along)
    return (16.0 * nearest - farther - 30.0 * field) / 12.0


def row_diff(wide, rows):
    nearest = wide[:, :, 1 : 1 + rows] + wide[:, :, 3 : 3 + rows]
    farther = wide[:, :, 0:rows] + wide[:, :, 4 : 4 + rows]
    return (16.0 * nearest - farther - 30.0 * wide[:, :, 2 : 2 + rows]) / 12.0


def hamiltonian(padded, potential, rows):
    wide = padded.astype(jnp.float32)
    field = wide[:, :, 2 : 2 + rows]
    laplace = second_diff(field, 1) + row_diff(wide, rows) + second_diff(field, 3)
    return (-0.5 * laplace + potential[None] * field).astype(jnp.bfloat16)


def local(
    orbitals, rotated_adj, level_adj, rotation, gap_inverse, potential, window_cols, tile_map
):
    local_orbs, planes, rows_y, cols_x = orbitals.shape
    cell_count = planes * rows_y * cols_x
    window_size = rotated_adj.shape[0]
    total_orbs = rotation.shape[0]
    orb_index = lax.axis_index("orb")
    tile_count = tile_map.shape[0]
    tile_size = total_orbs // tile_count
    local_tiles = local_orbs // tile_size
    owned_tiles = lax.dynamic_slice_in_dim(tile_map, orb_index * local_tiles, local_tiles)
    source_rows = (
        owned_tiles[:, None] * tile_size + jnp.arange(tile_size, dtype=jnp.int32)[None, :]
    ).reshape(local_orbs)
    stored = jnp.take(rotation, source_rows, axis=0)
    stored_wide = stored.astype(jnp.float32)
    right_factor = jnp.take(stored, window_cols, axis=1)
    flat_orbs = orbitals.reshape(local_orbs, cell_count)
    flat_adj = rotated_adj.reshape(window_size, cell_count)
    row_block = gap_inverse.shape[0]
    level_rows = orb_index * row_block + jnp.arange(row_block, dtype=jnp.int32)
    cell_dims = (((1,), (1,)), ((), ()))
    orb_dims = (((0,), (0,)), ((), ()))
    correlation = lax.psum(
        lax.dot_general(flat_orbs, flat_adj, cell_dims, preferred_element_type=jnp.float32), "grid"
    )
    partial_value = lax.dot_general(
        stored_wide, correlation, orb_dims, precision=lax.Precision.HIGHEST
    )
    coupling_in = lax.psum_scatter(partial_value, "orb", scatter_dimension=0, tiled=True)
    gap_cols = jnp.take(gap_inverse, window_cols, axis=1)
    diagonal = jnp.where(level_rows[:, None] == window_cols[None, :], level_adj[None, :], 0.0)
    coupling = gap_cols * coupling_in + diagonal
    coupling_all = lax.all_gather(coupling, "orb", axis=0, tiled=True)
    left_factor = jnp.dot(stored_wide, coupling_all, precision=lax.Precision.HIGHEST).astype(
        jnp.bfloat16
    )
    factors = jnp.concatenate([left_factor, right_factor], axis=1)
    field_terms = lax.dot_general(factors, flat_orbs, orb_dims, preferred_element_type=jnp.float32)
    combined = lax.psum(field_terms.astype(jnp.bfloat16), "orb")
    padded = padded_2(combined.reshape(2 * window_size, planes, rows_y, cols_x), (("grid", 2),), 2)
    applied = hamiltonian(padded, potential, rows_y)
    stacked = jnp.concatenate([flat_adj, applied.reshape(2 * window_size, cell_count)], axis=0)
    mix_coeffs = jnp.concatenate([right_factor, right_factor, left_factor], axis=1)
    result = jnp.dot(mix_coeffs, stacked, preferred_element_type=jnp.float32).astype(jnp.bfloat16)
    return result.reshape(orbitals.shape)


def solution(mesh):
    in_specs = (
        P("orb", None, "grid", None),
        P(None, None, "grid", None),
        P(),
        P(),
        P("orb", None),
        P(None, "grid", None),
        P(),
        P(),
    )
    out_specs = P("orb", None, "grid", None)
    return jax.shard_map(local, mesh=mesh, in_specs=in_specs, out_specs=out_specs, check_vma=False)
```

profile of v0, /device:TPU:1, one launch (start us, length us, event | category | flops | bytes accessed | tf_op | source)
XLA Modules:
  0.0 368.9 jit_solution(269607291713251803)
XLA Ops:
  6.5 4.8 %fusion.19 = f32[512,128]{1,0:T(8,128)} fusion(bf16[512,8,4,128]{3,2,1,0:T(4,128)(2,1)} %param.8, bf16[128,8,4,128]{3,2,1,0:T(4,128)(2,1)} %param.9), kind=kOutput, calls=%fused_computation.31 | convolution fusion | flops 536870912 | bytes 5505024 | tf_op jit(solution)/shard_map/dot_general | solution.py:64
  14.0 89.2 %all-reduce.3.cloned.1.call-done = f32[512,128]{1,0:T(8,128)} async-done(((f32[512,128]{1,0:T(8,128)}), f32[512,128]{1,0:T(8,128)}) %all-reduce.3.cloned.1.call-update) | async-done | bytes 262160 | tf_op jit(solution)/shard_map/psum | solution.py:63
  106.2 7.8 %reshape.69 = bf16[512,4096]{1,0:T(8,128)(2,1)} reshape(bf16[512,8,4,128]{3,2,1,0:T(4,128)(2,1)} %param.8) | data formatting | bytes 8388608 | tf_op jit(solution)/shard_map/reshape | solution.py:57
  114.0 2.9 copy.10
  121.5 8.2 %all_gather.3 = f32[1024,128]{0,1:T(8,128)S(1)} all-gather(f32[512,128]{0,1:T(8,128)S(1)} %fusion.31), channel_id=1, replica_groups=mesh['grid'=16,'orb'=2] {'orb'}, dimensions={0}, use_global_device_ids=true | all-gather | bytes 786432 | tf_op jit(solution)/shard_map/all_gather | solution.py:73
  130.9 3.4 convolution_convert_fusion.1
  134.4 2.7 reshape.70
  137.1 63.2 %all-reduce.5.cloned.1.call-done = bf16[256,8,4,128]{3,2,1,0:T(4,128)(2,1)} async-done(((bf16[256,8,4,128]{3,2,1,0:T(4,128)(2,1)}), bf16[256,8,4,128]{3,2,1,0:T(4,128)(2,1)}) %all-reduce.5.cloned.1.call-update) | async-done | bytes 2097168 | tf_op jit(solution)/shard_map/psum | solution.py:79
  200.3 5.0 %fusion.42 = (bf16[256,8,2,128]{3,2,1,0:T(2,128)(2,1)}, bf16[256,8,2,128]{3,2,1,0:T(2,128)(2,1)}) fusion(bf16[256,8,4,128]{3,2,1,0:T(4,128)(2,1)} %all-reduce.5.cloned.1.call-done), kind=kLoop, calls=%fused_computation.66 | loop fusion | bytes 4194304 | tf_op jit(solution)/shard_map/slice | solution.py:12
  207.1 2.6 reshape.68
  209.7 20.7 %collective-permute-done = bf16[256,8,2,128]{3,2,1,0:T(2,128)(2,1)S(1)} collective-permute-done((bf16[256,8,2,128]{3,2,1,0:T(2,128)(2,1)}, bf16[256,8,2,128]{3,2,1,0:T(2,128)(2,1)S(1)}, u32[]{:S(2)}, u32[]{:S(2)}) %collective-permute-start) | collective-permute-done | bytes 1048608 | tf_op jit(solution)/shard_map/ppermute | solution.py:14
  232.9 6.3 %maximum_convert_fusion = f32[256,8,8,128]{3,2,1,0:T(8,128)} fusion(bf16[256,8,2,128]{3,2,1,0:T(2,128)(2,1)} %collective-permute-done.1, bf16[256,8,4,128]{3,2,1,0:T(4,128)(2,1)S(1)} %copy-done.2, bf16[256,8,2,128]{3,2,1,0:T(2,128)(2,1)S(1)} %collective-permute-done), kind=kLoop, calls=%fused_computation.14 | loop fusion | flops 12582912 | bytes 12582912 | tf_op jit(solution)/shard_map/convert_element_type | solution.py:33
  239.2 11.4 %fusion.38 = (f32[256,8,4,1]{3,2,1,0:T(4,128)}, f32[256,8,4,1]{3,2,1,0:T(4,128)}) fusion(f32[256,8,8,128]{3,2,1,0:T(8,128)} %maximum_convert_fusion), kind=kLoop, calls=%fused_computation.62 | loop fusion | bytes 131072 | tf_op jit(solution)/shard_map/jit(_roll_static)/slice | solution.py:21
  250.6 11.3 %fusion.39 = (f32[256,8,4,127]{3,2,1,0:T(4,128)}, f32[256,8,4,127]{3,2,1,0:T(4,128)}) fusion(f32[256,8,8,128]{3,2,1,0:T(8,128)} %maximum_convert_fusion), kind=kLoop, calls=%fused_computation.63 | loop fusion | bytes 16646144 | tf_op jit(solution)/shard_map/jit(_roll_static)/slice | solution.py:21
  261.9 11.5 %fusion.40 = (f32[256,8,4,2]{3,2,1,0:T(4,128)}, f32[256,8,4,2]{3,2,1,0:T(4,128)}) fusion(f32[256,8,8,128]{3,2,1,0:T(8,128)} %maximum_convert_fusion), kind=kLoop, calls=%fused_computation.64 | loop fusion | bytes 262144 | tf_op jit(solution)/shard_map/jit(_roll_static)/slice | solution.py:22
  273.4 11.4 %fusion.41 = (f32[256,8,4,126]{3,2,1,0:T(4,128)}, f32[256,8,4,126]{3,2,1,0:T(4,128)}) fusion(f32[256,8,8,128]{3,2,1,0:T(8,128)} %maximum_convert_fusion), kind=kLoop, calls=%fused_computation.65 | loop fusion | bytes 16515072 | tf_op jit(solution)/shard_map/jit(_roll_static)/slice | solution.py:22
  284.8 9.7 %fusion.35 = (f32[256,7,4,128]{3,2,1,0:T(4,128)}, f32[256,7,4,128]{3,2,1,0:T(4,128)}) fusion(f32[256,8,8,128]{3,2,1,0:T(8,128)} %maximum_convert_fusion), kind=kLoop, calls=%fused_computation.59 | loop fusion | bytes 14680064 | tf_op jit(solution)/shard_map/jit(_roll_static)/slice | solution.py:21
  294.5 8.7 %fusion.37 = (f32[256,6,4,128]{3,2,1,0:T(4,128)}, f32[256,6,4,128]{3,2,1,0:T(4,128)}) fusion(f32[256,8,8,128]{3,2,1,0:T(8,128)} %maximum_convert_fusion), kind=kLoop, calls=%fused_computation.61 | loop fusion | bytes 12582912 | tf_op jit(solution)/shard_map/jit(_roll_static)/slice | solution.py:22
  303.2 2.7 fusion.36
  305.9 2.6 fusion.34
  308.5 37.3 %fusion.15 = bf16[256,8,4,128]{3,2,1,0:T(4,128)(2,1)S(1)} fusion(f32[256,8,4,2]{3,2,1,0:T(4,128)} %get-tuple-element.18, f32[256,8,4,126]{3,2,1,0:T(4,128)} %get-tuple-element.20, f32[256,8,4,126]{3,2,1,0:T(4,128)} %get-tuple-element.19, f32[256,8,4,2]{3,2,1,0:T(4,128)} %get-tuple-element.17, f32[256,8,4,1]{3,2,1,0:T(4,128)} %get-tuple-element.14, ...), kind=kLoop, calls=%fused_computation.27 | loop fusion | flops 31457280 | bytes 56639488 | tf_op jit(solution)/shard_map/convert_element_type | solution.py:36
  345.8 2.8 reshape.71
  348.6 6.1 %convolution_convert_fusion = bf16[512,4096]{1,0:T(8,128)(2,1)} fusion(bf16[256,4096]{1,0:T(8,128)(2,1)} %reshape.71, bf16[128,4096]{1,0:T(8,128)(2,1)S(1)} %copy-done.3, bf16[512,128]{0,1:T(8,128)(2,1)S(1)} %convolution_convert_fusion.2, bf16[512,128]{0,1:T(8,128)(2,1)S(1)} %select_bitcast_fusion), kind=kOutput, calls=%fused_computation.3 | convolution fusion | flops 1620180992 | bytes 7602176 | tf_op jit(solution)/shard_map/dot_general | solution.py:84
  354.7 7.7 %reshape.72 = bf16[512,8,4,128]{3,2,1,0:T(4,128)(2,1)} reshape(bf16[512,4096]{1,0:T(8,128)(2,1)} %convolution_convert_fusion) | data formatting | bytes 8388608 | tf_op jit(solution)/shard_map/reshape | solution.py:85
  (44 shorter events, 15.5 us)
Async XLA Ops:
  6.5 5.2 %copy-start = (bf16[1024,1024]{1,0:T(8,128)(2,1)S(1)}, bf16[1024,1024]{1,0:T(8,128)(2,1)}, u32[]{:S(2)}) copy-start(bf16[1024,1024]{1,0:T(8,128)(2,1)} %param.11) | copy-start | bytes 6291460
  6.5 4.9 %copy-start.7 = (s32[8]{0:T(128)S(1)}, s32[8]{0:T(128)}, u32[]{:S(2)}) copy-start(s32[8]{0:T(128)} %param.15) | copy-start | bytes 100
  6.5 96.6 %all-reduce.3.cloned.1.call-start = ((), (), s32[]{:S(2)}) async-start(), calls=%async_computation.1 | async-start | bytes 524288 | tf_op jit(solution)/shard_map/psum | solution.py:63
  11.4 109.0 %reduce-scatter.2.cloned.1.call-start = ((), (), s32[]{:S(2)}) async-start(), calls=%async_computation.2 | async-start | bytes 786432 | tf_op jit(solution)/shard_map/reduce_scatter | solution.py:69
  105.6 94.7 %all-reduce.5.cloned.1.call-start = ((), (), s32[]{:S(2)}) async-start(), calls=%async_computation.3 | async-start | bytes 4194304 | tf_op jit(solution)/shard_map/psum | solution.py:79
  114.0 2.9 copy-start.5
  114.0 6.4 %copy-start.6 = (f32[128]{0:T(128)S(1)}, f32[128]{0:T(128)}, u32[]{:S(2)}) copy-start(f32[128]{0:T(128)} %param.10) | copy-start | bytes 1540
  200.3 32.6 %copy-start.2 = (bf16[256,8,4,128]{3,2,1,0:T(4,128)(2,1)S(1)}, bf16[256,8,4,128]{3,2,1,0:T(4,128)(2,1)}, u32[]{:S(2)}) copy-start(bf16[256,8,4,128]{3,2,1,0:T(4,128)(2,1)} %all-reduce.5.cloned.1.call-done) | copy-start | bytes 6291460
  205.4 25.0 %collective-permute-start = (bf16[256,8,2,128]{3,2,1,0:T(2,128)(2,1)}, bf16[256,8,2,128]{3,2,1,0:T(2,128)(2,1)S(1)}, u32[]{:S(2)}, u32[]{:S(2)}) collective-permute-start(bf16[256,8,2,128]{3,2,1,0:T(2,128)(2,1)} %get-tuple-element.21), channel_id=1, source_target_pairs={{0,2},{2,4},{4,6},{6,8},{8,10},{10,12},{12,14},{14,16},{16,18},{18... | collective-permute-start | bytes 3145736 | tf_op jit(solution)/shard_map/ppermute | solution.py:14
  207.1 25.8 %collective-permute-start.1 = (bf16[256,8,2,128]{3,2,1,0:T(2,128)(2,1)}, bf16[256,8,2,128]{3,2,1,0:T(2,128)(2,1)}, u32[]{:S(2)}, u32[]{:S(2)}) collective-permute-start(bf16[256,8,2,128]{3,2,1,0:T(2,128)(2,1)} %get-tuple-element.22), channel_id=1, source_target_pairs={{2,0},{4,2},{6,4},{8,6},{10,8},{12,10},{14,12},{16,14},{18,16},{20... | collective-permute-start | bytes 3145736 | tf_op jit(solution)/shard_map/ppermute | solution.py:15
  303.2 5.3 %copy-start.4 = (f32[8,4,128]{2,1,0:T(4,128)S(1)}, f32[8,4,128]{2,1,0:T(4,128)}, u32[]{:S(2)}) copy-start(f32[8,4,128]{2,1,0:T(4,128)} %param.13) | copy-start | bytes 49156
  345.8 2.8 copy-start.3
  348.6 13.8 %copy-start.1 = (bf16[1024,1024]{1,0:T(8,128)(2,1)S(1)}, bf16[1024,1024]{1,0:T(8,128)(2,1)}, u32[]{:S(2)}) copy-start(bf16[1024,1024]{1,0:T(8,128)(2,1)} %param.11) | copy-start | bytes 6291460
Sparse Core Ops, SparseCore 0:
  11.5 91.5 all-reduce.2
  105.7 14.3 reduce-scatter.1
  137.2 63.0 all-reduce.4
where the time goes:
time: 370 us; the launch traced here: 369 us
  waiting for transfers between devices  176 us (48%)
  local copies, waits for them, and re-layouts  107 us (29%)
  other arithmetic  45.2 us (12%)
  matrix products  17.9 us (5%)
  between operations  13.3 us (4%)
  blocking collectives  8.24 us (2%)
    psum x1, waiting for transfers between devices, local(): lax.psum(lax.dot_general(flat_orbs, flat_adj, cell_dims, preferred_elemen...  89.2 us
    psum x1, waiting for transfers between devices, local(): combined = lax.psum(field_terms.astype(jnp.bfloat16), 'orb')  63.2 us
    convert_element_type x1, other arithmetic, hamiltonian(): return (-0.5 * laplace + potential[None] * field).astype(jnp.bfloat16)  37.3 us
    slice x4, local copies, waits for them, and re-layouts, second_diff(): nearest = jnp.roll(field, 1, along) + jnp.roll(field, -1, along)  35 us
    slice x4, local copies, waits for them, and re-layouts, second_diff(): farther = jnp.roll(field, 2, along) + jnp.roll(field, -2, along)  34.3 us
    ppermute x1, waiting for transfers between devices, padded_2(): before = lax.ppermute(last, axis, up)  20.7 us
    all_gather x1, blocking collectives, local(): coupling_all = lax.all_gather(coupling, 'orb', axis=0, tiled=True)  8.24 us
    reshape x1, local copies, waits for them, and re-layouts, local(): flat_orbs = orbitals.reshape(local_orbs, cell_count)  7.81 us
  transfers between devices with their start and end apart: 5, of which 4 were waited for; matrix products, arithmetic and copies ran while one was open for 5% of the time, Pallas kernels for 0%

commit v1 on v0

v1 whole, which is shorter than its diff:
```python
import functools

import jax
import jax.numpy as jnp
from jax import lax
from jax.experimental import pallas as pl
from jax.experimental.pallas import tpu as pltpu
from jax.sharding import PartitionSpec as P

MESH = pl.DeviceIdType.MESH
NCH = 4
F32 = jnp.float32
BF16 = jnp.bfloat16
NT = (((1,), (1,)), ((), ()))
NN = (((1,), (0,)), ((), ()))


def dot(a, b, dims):
    return lax.dot_general(a, b, dims, preferred_element_type=F32)


def split3(x):
    hi = x.astype(BF16)
    rest = x - hi.astype(F32)
    mid = rest.astype(BF16)
    low = (rest - mid.astype(F32)).astype(BF16)
    return hi, mid, low


def fields_kernel(
    n, planes, rows,
    orb_ref, adj_ref, stored_ref, gap_ref, level_ref, cols_ref, pot_ref,
    app_ref, fac_ref,
    corr, rs_buf, ag_buf, gap_all, part, peer, wide,
    rs_send, rs_recv, ag_send, ag_recv, gap_send, gap_recv,
    sum_send, sum_recv, up_send, up_recv, down_send, down_recv,
):
    slabs, local_orbs, nx = orb_ref.shape
    w = adj_ref.shape[1]
    norb = stored_ref.shape[0]
    chunk = local_orbs // n
    wc = w // NCH
    total = 2 * n
    g = lax.axis_index("grid")
    o = lax.axis_index("orb")
    me = o * n + g
    other = 1 - o
    after = lax.rem(g + 1, n)
    before = lax.rem(g + n - 1, n)

    barrier = pltpu.get_barrier_semaphore()

    def greet(k, _):
        to = lax.rem(me + k, total)
        pl.semaphore_signal(
            barrier, inc=1, device_id=(lax.rem(to, n), to // n), device_id_type=MESH
        )
        return 0

    lax.fori_loop(1, total, greet, 0)

    corr[...] = jnp.zeros_like(corr)

    def corr_step(r, _):
        corr[...] += dot(orb_ref[r], adj_ref[r], NT).reshape(corr.shape)
        return 0

    lax.fori_loop(0, slabs, corr_step, 0)
    pl.semaphore_wait(barrier, total - 1)

    def rs_copy(k):
        to = lax.rem(g + k, n)
        return pltpu.make_async_remote_copy(
            src_ref=corr.at[to], dst_ref=rs_buf.at[k],
            send_sem=rs_send.at[k], recv_sem=rs_recv.at[k],
            device_id=(to, o), device_id_type=MESH,
        )

    def rs_start(k, _):
        rs_copy(k).start()
        return 0

    lax.fori_loop(1, n, rs_start, 0)

    def sum_copy(half, ch):
        i = half * NCH + ch
        return pltpu.make_async_remote_copy(
            src_ref=part.at[i], dst_ref=peer.at[i],
            send_sem=sum_send.at[i], recv_sem=sum_recv.at[i],
            device_id=(g, other), device_id_type=MESH,
        )

    def up_copy(half, ch):
        i = half * NCH + ch
        return pltpu.make_async_remote_copy(
            src_ref=wide.at[i, pl.ds(rows, 2)], dst_ref=wide.at[i, pl.ds(0, 2)],
            send_sem=up_send.at[i], recv_sem=up_recv.at[i],
            device_id=(after, o), device_id_type=MESH,
        )

    def down_copy(half, ch):
        i = half * NCH + ch
        return pltpu.make_async_remote_copy(
            src_ref=wide.at[i, pl.ds(2, 2)], dst_ref=wide.at[i, pl.ds(rows + 2, 2)],
            send_sem=down_send.at[i], recv_sem=down_recv.at[i],
            device_id=(before, o), device_id_type=MESH,
        )

    def send_partials(half, factor_t):
        def step(r, _):
            term = dot(factor_t, orb_ref[r], NN).astype(BF16)
            for ch in range(NCH):
                part[half * NCH + ch, r] = term[ch * wc : (ch + 1) * wc]
            return 0

        lax.fori_loop(0, slabs, step, 0)
        for ch in range(NCH):
            sum_copy(half, ch).start()

    mine = pl.ds(pl.multiple_of(o * local_orbs, local_orbs), local_orbs)
    level_rows = lax.broadcasted_iota(jnp.int32, (w, norb), 1)
    hot = level_rows == cols_ref[...]
    hot16 = hot.astype(F32).astype(BF16)
    right_t = dot(hot16, stored_ref[mine, :], NT).astype(BF16)
    fac_ref[0] = right_t
    send_partials(0, right_t)

    hi, mid, low = split3(gap_ref[...])
    gap_all[o] = dot(hot16, hi, NT) + dot(hot16, mid, NT) + dot(hot16, low, NT)
    gap_copy = pltpu.make_async_remote_copy(
        src_ref=gap_all.at[o], dst_ref=gap_all.at[o],
        send_sem=gap_send, recv_sem=gap_recv,
        device_id=(g, other), device_id_type=MESH,
    )
    gap_copy.start()

    ag_buf[me] = corr[g]

    def rs_take(k, _):
        rs_copy(k).wait_recv()
        ag_buf[me] += rs_buf[k]
        return 0

    lax.fori_loop(1, n, rs_take, 0)

    def ag_copy(k):
        to = lax.rem(me + k, total)
        return pltpu.make_async_remote_copy(
            src_ref=ag_buf.at[me], dst_ref=ag_buf.at[me],
            send_sem=ag_send.at[k], recv_sem=ag_recv.at[k],
            device_id=(lax.rem(to, n), to // n), device_id_type=MESH,
        )

    def ag_start(k, _):
        ag_copy(k).start()
        return 0

    def ag_take(k, _):
        ag_copy(k).wait_recv()
        return 0

    lax.fori_loop(1, total, ag_start, 0)
    lax.fori_loop(1, total, ag_take, 0)
    gap_copy.wait_recv()

    corr_t = ag_buf[...].reshape(norb, w).T
    parts_t = jnp.concatenate(split3(corr_t), axis=0)
    rotated = dot(parts_t, stored_ref[...], NN)
    coupling_in = rotated[:w] + rotated[w : 2 * w] + rotated[2 * w :]
    gap_cols = jnp.concatenate([gap_all[0], gap_all[1]], axis=1)
    coupling = gap_cols * coupling_in + jnp.where(hot, level_ref[...], 0.0)
    mixed = dot(jnp.concatenate(split3(coupling), axis=0), stored_ref[mine, :], NT)
    left_t = (mixed[:w] + mixed[w : 2 * w] + mixed[2 * w :]).astype(BF16)
    fac_ref[1] = left_t
    send_partials(1, left_t)

    def combine(half, ch):
        i = half * NCH + ch
        sum_copy(half, ch).wait_recv()

        def step(p, _):
            for y in range(rows):
                r = p * rows + y
                wide[i, 2 + y, p] = (
                    part[i, r].astype(F32) + peer[i, r].astype(F32)
                ).astype(BF16)
            return 0

        lax.fori_loop(0, planes, step, 0)
        up_copy(half, ch).start()
        down_copy(half, ch).start()

    def stencil(half, ch):
        i = half * NCH + ch
        up_copy(half, ch).wait_recv()
        down_copy(half, ch).wait_recv()

        def step(p, _):
            lines = [wide[i, y, p].astype(F32) for y in range(rows + 4)]
            near_planes = [lax.rem(p + d, planes) for d in (1, planes - 1)]
            far_planes = [lax.rem(p + d, planes) for d in (2, planes - 2)]
            for y in range(rows):
                f = lines[y + 2]
                near = lines[y + 1] + lines[y + 3]
                far = lines[y] + lines[y + 4]
                for q in near_planes:
                    near = near + wide[i, 2 + y, q].astype(F32)
                for q in far_planes:
                    far = far + wide[i, 2 + y, q].astype(F32)
                near = near + pltpu.roll(f, 1, 1) + pltpu.roll(f, nx - 1, 1)
                far = far + pltpu.roll(f, 2, 1) + pltpu.roll(f, nx - 2, 1)
                r = p * rows + y
                diag = 3.75 + pot_ref[pl.ds(r, 1), :]
                value = diag * f - (2.0 / 3.0) * near + (1.0 / 24.0) * far
                app_ref[r, half * w + ch * wc : half * w + (ch + 1) * wc] = value.astype(BF16)
            return 0

        lax.fori_loop(0, planes, step, 0)

    for half in range(2):
        for ch in range(NCH):
            combine(half, ch)
            if ch:
                stencil(half, ch - 1)
        stencil(half, NCH - 1)

    def rs_done(k, _):
        rs_copy(k).wait_send()
        return 0

    def ag_done(k, _):
        ag_copy(k).wait_send()
        return 0

    lax.fori_loop(1, n, rs_done, 0)
    lax.fori_loop(1, total, ag_done, 0)
    gap_copy.wait_send()
    for half in range(2):
        for ch in range(NCH):
            sum_copy(half, ch).wait_send()
            up_copy(half, ch).wait_send()
            down_copy(half, ch).wait_send()


def local(
    orbitals, rotated_adj, level_adj, rotation, gap_inverse, potential, window_cols, tile_map
):
    local_orbs, planes, rows, nx = orbitals.shape
    w = rotated_adj.shape[0]
    norb = rotation.shape[0]
    tiles = tile_map.shape[0]
    n = lax.axis_size("grid")
    slabs = planes * rows
    chunk = local_orbs // n
    wc = w // NCH
    orb_r = orbitals.reshape(local_orbs, slabs, nx).transpose(1, 0, 2)
    adj_r = rotated_adj.reshape(w, slabs, nx).transpose(1, 0, 2)
    stored = jnp.take(
        rotation.reshape(tiles, norb // tiles, norb), tile_map, axis=0, mode="clip"
    ).reshape(norb, norb)
    vmem = pl.BlockSpec(memory_space=pltpu.VMEM)
    dma = pltpu.SemaphoreType.DMA
    applied, factors = pl.pallas_call(
        functools.partial(fields_kernel, n, planes, rows),
        out_shape=(
            jax.ShapeDtypeStruct((slabs, 2 * w, nx), BF16),
            jax.ShapeDtypeStruct((2, w, local_orbs), BF16),
        ),
        in_specs=[vmem] * 7,
        out_specs=(vmem, vmem),
        scratch_shapes=[
            pltpu.VMEM((n, chunk, w), F32),
            pltpu.VMEM((n, chunk, w), F32),
            pltpu.VMEM((2 * n, chunk, w), F32),
            pltpu.VMEM((2, w, local_orbs), F32),
            pltpu.VMEM((2 * NCH, slabs, wc, nx), BF16),
            pltpu.VMEM((2 * NCH, slabs, wc, nx), BF16),
            pltpu.VMEM((2 * NCH, rows + 4, planes, wc, nx), BF16),
            dma((n,)), dma((n,)), dma((2 * n,)), dma((2 * n,)), dma, dma,
            dma((2 * NCH,)), dma((2 * NCH,)), dma((2 * NCH,)),
            dma((2 * NCH,)), dma((2 * NCH,)), dma((2 * NCH,)),
        ],
        compiler_params=pltpu.CompilerParams(
            collective_id=0, has_side_effects=True, vmem_limit_bytes=56 * 1024 * 1024
        ),
    )(
        orb_r, adj_r, stored, gap_inverse, level_adj.reshape(w, 1),
        window_cols.reshape(w, 1), potential.reshape(slabs, nx),
    )
    stacked = jnp.concatenate([adj_r, applied], axis=1)
    mix_t = jnp.concatenate([factors[0], factors[1], factors[0]], axis=0)
    result = lax.dot_general(
        mix_t, stacked, (((0,), (1,)), ((), ())), preferred_element_type=F32
    ).astype(BF16)
    return result.reshape(orbitals.shape)


def solution(mesh):
    in_specs = (
        P("orb", None, "grid", None),
        P(None, None, "grid", None),
        P(),
        P(),
        P("orb", None),
        P(None, "grid", None),
        P(),
        P(),
    )
    out_specs = P("orb", None, "grid", None)
    return jax.shard_map(local, mesh=mesh, in_specs=in_specs, out_specs=out_specs, check_vma=False)
```

time: 370 us -> 121 us (0.33)
  the two profiles are of different devices: /device:TPU:1 before, /device:TPU:0 now
where the time goes in v1:
time: 121 us
  Pallas kernels  95.5 us (79%)
  local copies, waits for them, and re-layouts  21 us (17%)
  matrix products  3.98 us (3%)
    pallas_call x1, Pallas kernels, local(): pl.pallas_call(functools.partial(fields_kernel, n, planes, rows), out_sha...  95.5 us
    unnamed x6, local copies, waits for them, and re-layouts  10 us
    reshape x1, local copies, waits for them, and re-layouts, local(): return result.reshape(orbitals.shape)  5.25 us
    dot_general x1, matrix products, local(): lax.dot_general(mix_t, stacked, (((0,), (1,)), ((), ())), preferred_eleme...  3.98 us

profile of v1, /device:TPU:0, one launch (start us, length us, event | category | flops | bytes accessed | tf_op | source)
XLA Modules:
  0.0 121.2 jit_solution(15825927512710665997)
XLA Ops:
  0.0 0.0 copy-start
  0.0 1.6 %copy-done = bf16[1024,1024]{1,0:T(8,128)(2,1)S(1)} copy-done((bf16[1024,1024]{1,0:T(8,128)(2,1)S(1)}, bf16[1024,1024]{1,0:T(8,128)(2,1)}, u32[]{:S(2)}) %copy-start) | copy-done | bytes 2097176
  1.6 0.7 pad_clamp_fusion
  2.3 1.4 %copy.11.level_ref = f32[128,1]{1,0:T(8,128)} copy(f32[128,1]{0,1:T(1,128)} %bitcast.26) | data formatting | bytes 1024 | tf_op jit(solution)/shard_map/reshape | solution.py:287
  3.6 1.4 %copy.12.cols_ref = s32[128,1]{1,0:T(8,128)} copy(s32[128,1]{0,1:T(1,128)} %bitcast.27) | data formatting | bytes 1024 | tf_op jit(solution)/shard_map/reshape | solution.py:288
  5.0 2.6 %copy.10 = bf16[128,8,4,128]{3,0,2,1:T(8,128)(2,1)} copy(bf16[128,8,4,128]{3,2,1,0:T(4,128)(2,1)} %param.9) | data formatting | bytes 2097152 | tf_op args[1]
  7.6 2.0 %gather_fusion = bf16[8,128,1024]{2,1,0:T(8,128)(2,1)} fusion(bf16[8,128,1024]{2,1,0:T(8,128)(2,1)S(1)} %bitcast.19, s32[1024]{0:T(1024)S(1)} %pad_clamp_fusion), kind=kCustom, calls=%fused_computation | custom fusion | bytes 4194336 | tf_op jit(solution)/shard_map/jit(_take)/gather | solution.py:258
  9.6 5.8 %copy.9 = bf16[512,8,4,128]{3,0,2,1:T(8,128)(2,1)} copy(bf16[512,8,4,128]{3,2,1,0:T(4,128)(2,1)} %param.8) | data formatting | bytes 8388608 | tf_op args[0]
  15.4 0.0 copy-start.1
  15.4 95.5 %shard_map.82 = (bf16[32,256,128]{2,1,0:T(8,128)(2,1)}, bf16[2,128,512]{2,1,0:T(8,128)(2,1)}) custom-call(bf16[32,512,128]{2,1,0:T(8,128)(2,1)} %bitcast.20, bf16[32,128,128]{2,1,0:T(8,128)(2,1)} %bitcast.22, bf16[1024,1024]{1,0:T(8,128)(2,1)} %bitcast.21, f32[512,1024]{1,0:T(8,128)} %gap_ref.1, f32[128,1]{1,0:T(8,128)} %copy.11.level_ref, ...), custom_call_target="tpu_custom_call" | custom-call | tf_op jit(solution)/shard_map/pallas_call | solution.py:263
  110.9 1.0 slice_bitcast_fusion
  111.9 0.0 copy-done.1
  111.9 4.0 %fusion.4 = bf16[512,32,128]{2,0,1:T(8,128)(2,1)S(1)} fusion(bf16[32,256,128]{2,1,0:T(8,128)(2,1)} %get-tuple-element.8, bf16[32,128,128]{2,1,0:T(8,128)(2,1)S(1)} %bitcast.23, bf16[128,512]{1,0:T(8,128)(2,1)S(1)} %get-tuple-element.10, bf16[128,512]{1,0:T(8,128)(2,1)S(1)} %get-tuple-element.9), kind=kOutput, calls=%fused_computation.5 | convolution fusion | flops 1620180992 | bytes 7602176 | tf_op jit(solution)/shard_map/dot_general | solution.py:292
  115.9 5.2 %copy.14 = bf16[512,8,4,128]{3,2,1,0:T(4,128)(2,1)} copy(bf16[512,8,4,128]{3,0,2,1:T(8,128)(2,1)S(1)} %bitcast.24) | data formatting | bytes 8388608 | tf_op jit(solution)/shard_map/reshape | solution.py:295
Async XLA Ops:
  0.0 1.6 %copy-start = (bf16[1024,1024]{1,0:T(8,128)(2,1)S(1)}, bf16[1024,1024]{1,0:T(8,128)(2,1)}, u32[]{:S(2)}) copy-start(bf16[1024,1024]{1,0:T(8,128)(2,1)} %param.11) | copy-start | bytes 6291460
  15.4 96.5 %copy-start.1 = (bf16[128,8,4,128]{3,0,2,1:T(8,128)(2,1)S(1)}, bf16[128,8,4,128]{3,0,2,1:T(8,128)(2,1)}, u32[]{:S(2)}) copy-start(bf16[128,8,4,128]{3,0,2,1:T(8,128)(2,1)} %copy.10) | copy-start | bytes 3145732

commit v2 on v1

--- a/solution.py
+++ b/solution.py
@@ -8,7 +8,8 @@
 from jax.sharding import PartitionSpec as P
 
 MESH = pl.DeviceIdType.MESH
-NCH = 4
+NCH = 8
+EARLY = 2
 F32 = jnp.float32
 BF16 = jnp.bfloat16
 NT = (((1,), (1,)), ((), ()))
@@ -38,9 +39,7 @@
     slabs, local_orbs, nx = orb_ref.shape
     w = adj_ref.shape[1]
     norb = stored_ref.shape[0]
-    chunk = local_orbs // n
     wc = w // NCH
-    total = 2 * n
     g = lax.axis_index("grid")
     o = lax.axis_index("orb")
     me = o * n + g
@@ -51,22 +50,13 @@
     barrier = pltpu.get_barrier_semaphore()
 
     def greet(k, _):
-        to = lax.rem(me + k, total)
         pl.semaphore_signal(
-            barrier, inc=1, device_id=(lax.rem(to, n), to // n), device_id_type=MESH
-        )
-        return 0
-
-    lax.fori_loop(1, total, greet, 0)
-
-    corr[...] = jnp.zeros_like(corr)
-
-    def corr_step(r, _):
-        corr[...] += dot(orb_ref[r], adj_ref[r], NT).reshape(corr.shape)
-        return 0
-
-    lax.fori_loop(0, slabs, corr_step, 0)
-    pl.semaphore_wait(barrier, total - 1)
+            barrier, inc=1, device_id=(lax.rem(g + k, n), o), device_id_type=MESH
+        )
+        return 0
+
+    pl.semaphore_signal(barrier, inc=1, device_id=(g, other), device_id_type=MESH)
+    lax.fori_loop(1, n, greet, 0)
 
     def rs_copy(k):
         to = lax.rem(g + k, n)
@@ -80,8 +70,6 @@
         rs_copy(k).start()
         return 0
 
-    lax.fori_loop(1, n, rs_start, 0)
-
     def sum_copy(half, ch):
         i = half * NCH + ch
         return pltpu.make_async_remote_copy(
@@ -106,24 +94,29 @@
             device_id=(before, o), device_id_type=MESH,
         )
 
-    def send_partials(half, factor_t):
-        def step(r, _):
-            term = dot(factor_t, orb_ref[r], NN).astype(BF16)
+    def partials(half, factor_t):
+        def step(k, _):
+            pair = jnp.concatenate([orb_ref[2 * k], orb_ref[2 * k + 1]], axis=1)
+            term = dot(factor_t, pair, NN).astype(BF16)
             for ch in range(NCH):
-                part[half * NCH + ch, r] = term[ch * wc : (ch + 1) * wc]
+                fields = term[ch * wc : (ch + 1) * wc]
+                part[half * NCH + ch, 2 * k] = fields[:, :nx]
+                part[half * NCH + ch, 2 * k + 1] = fields[:, nx:]
             return 0
 
-        lax.fori_loop(0, slabs, step, 0)
-        for ch in range(NCH):
-            sum_copy(half, ch).start()
+        lax.fori_loop(0, slabs // 2, step, 0)
+
+    def column(row_ref):
+        row = row_ref[...].astype(F32)
+        return jnp.broadcast_to(row, (w, w)).T[:, :1]
 
     mine = pl.ds(pl.multiple_of(o * local_orbs, local_orbs), local_orbs)
-    level_rows = lax.broadcasted_iota(jnp.int32, (w, norb), 1)
-    hot = level_rows == cols_ref[...]
+    level_rows = lax.broadcasted_iota(jnp.int32, (w, norb), 1).astype(F32)
+    hot = level_rows == column(cols_ref)
     hot16 = hot.astype(F32).astype(BF16)
     right_t = dot(hot16, stored_ref[mine, :], NT).astype(BF16)
     fac_ref[0] = right_t
-    send_partials(0, right_t)
+    fac_ref[2] = right_t
 
     hi, mid, low = split3(gap_ref[...])
     gap_all[o] = dot(hot16, hi, NT) + dot(hot16, mid, NT) + dot(hot16, low, NT)
@@ -132,7 +125,28 @@
         send_sem=gap_send, recv_sem=gap_recv,
         device_id=(g, other), device_id_type=MESH,
     )
+    pl.semaphore_wait(barrier, n)
     gap_copy.start()
+    partials(0, right_t)
+    for ch in range(EARLY):
+        sum_copy(0, ch).start()
+
+    corr[...] = jnp.zeros_like(corr)
+
+    def corr_step(k, _):
+        orbs = jnp.concatenate([orb_ref[4 * k + i] for i in range(4)], axis=1)
+        adjs = jnp.concatenate([adj_ref[4 * k + i] for i in range(4)], axis=1)
+        corr[...] += dot(orbs, adjs, NT).reshape(corr.shape)
+        return 0
+
+    lax.fori_loop(0, slabs // 4, corr_step, 0)
+    lax.fori_loop(1, n, rs_start, 0)
+
+    def stack_step(r, _):
+        app_ref[r, :w] = adj_ref[r]
+        return 0
+
+    lax.fori_loop(0, slabs, stack_step, 0)
 
     ag_buf[me] = corr[g]
 
@@ -143,24 +157,40 @@
 
     lax.fori_loop(1, n, rs_take, 0)
 
-    def ag_copy(k):
-        to = lax.rem(me + k, total)
-        return pltpu.make_async_remote_copy(
-            src_ref=ag_buf.at[me], dst_ref=ag_buf.at[me],
-            send_sem=ag_send.at[k], recv_sem=ag_recv.at[k],
-            device_id=(lax.rem(to, n), to // n), device_id_type=MESH,
+    theirs = other * n + g
+    cross_copy = pltpu.make_async_remote_copy(
+        src_ref=ag_buf.at[me], dst_ref=ag_buf.at[me],
+        send_sem=ag_send.at[0], recv_sem=ag_recv.at[0],
+        device_id=(g, other), device_id_type=MESH,
+    )
+
+    def ag_copy(k, slot, first):
+        return pltpu.make_async_remote_copy(
+            src_ref=ag_buf.at[slot], dst_ref=ag_buf.at[slot],
+            send_sem=ag_send.at[first + k], recv_sem=ag_recv.at[first + k],
+            device_id=(lax.rem(g + k, n), o), device_id_type=MESH,
         )
 
     def ag_start(k, _):
-        ag_copy(k).start()
+        ag_copy(k, me, 0).start()
+        return 0
+
+    def ag_forward(k, _):
+        ag_copy(k, theirs, n).start()
         return 0
 
     def ag_take(k, _):
-        ag_copy(k).wait_recv()
-        return 0
-
-    lax.fori_loop(1, total, ag_start, 0)
-    lax.fori_loop(1, total, ag_take, 0)
+        ag_copy(k, me, 0).wait_recv()
+        ag_copy(k, theirs, n).wait_recv()
+        return 0
+
+    cross_copy.start()
+    lax.fori_loop(1, n, ag_start, 0)
+    for ch in range(EARLY, NCH):
+        sum_copy(0, ch).start()
+    cross_copy.wait_recv()
+    lax.fori_loop(1, n, ag_forward, 0)
+    lax.fori_loop(1, n, ag_take, 0)
     gap_copy.wait_recv()
 
     corr_t = ag_buf[...].reshape(norb, w).T
@@ -168,11 +198,13 @@
     rotated = dot(parts_t, stored_ref[...], NN)
     coupling_in = rotated[:w] + rotated[w : 2 * w] + rotated[2 * w :]
     gap_cols = jnp.concatenate([gap_all[0], gap_all[1]], axis=1)
-    coupling = gap_cols * coupling_in + jnp.where(hot, level_ref[...], 0.0)
+    coupling = gap_cols * coupling_in + jnp.where(hot, column(level_ref), 0.0)
     mixed = dot(jnp.concatenate(split3(coupling), axis=0), stored_ref[mine, :], NT)
     left_t = (mixed[:w] + mixed[w : 2 * w] + mixed[2 * w :]).astype(BF16)
     fac_ref[1] = left_t
-    send_partials(1, left_t)
+    partials(1, left_t)
+    for ch in range(NCH):
+        sum_copy(1, ch).start()
 
     def combine(half, ch):
         i = half * NCH + ch
@@ -194,6 +226,7 @@
         i = half * NCH + ch
         up_copy(half, ch).wait_recv()
         down_copy(half, ch).wait_recv()
+        first = (half + 1) * w + ch * wc
 
         def step(p, _):
             lines = [wide[i, y, p].astype(F32) for y in range(rows + 4)]
@@ -212,7 +245,7 @@
                 r = p * rows + y
                 diag = 3.75 + pot_ref[pl.ds(r, 1), :]
                 value = diag * f - (2.0 / 3.0) * near + (1.0 / 24.0) * far
-                app_ref[r, half * w + ch * wc : half * w + (ch + 1) * wc] = value.astype(BF16)
+                app_ref[r, first : first + wc] = value.astype(BF16)
             return 0
 
         lax.fori_loop(0, planes, step, 0)
@@ -229,11 +262,13 @@
         return 0
 
     def ag_done(k, _):
-        ag_copy(k).wait_send()
+        ag_copy(k, me, 0).wait_send()
+        ag_copy(k, theirs, n).wait_send()
         return 0
 
     lax.fori_loop(1, n, rs_done, 0)
-    lax.fori_loop(1, total, ag_done, 0)
+    lax.fori_loop(1, n, ag_done, 0)
+    cross_copy.wait_send()
     gap_copy.wait_send()
     for half in range(2):
         for ch in range(NCH):
@@ -248,23 +283,23 @@
     local_orbs, planes, rows, nx = orbitals.shape
     w = rotated_adj.shape[0]
     norb = rotation.shape[0]
-    tiles = tile_map.shape[0]
     n = lax.axis_size("grid")
     slabs = planes * rows
     chunk = local_orbs // n
     wc = w // NCH
     orb_r = orbitals.reshape(local_orbs, slabs, nx).transpose(1, 0, 2)
     adj_r = rotated_adj.reshape(w, slabs, nx).transpose(1, 0, 2)
+    tiles = tile_map.shape[0]
     stored = jnp.take(
         rotation.reshape(tiles, norb // tiles, norb), tile_map, axis=0, mode="clip"
     ).reshape(norb, norb)
     vmem = pl.BlockSpec(memory_space=pltpu.VMEM)
     dma = pltpu.SemaphoreType.DMA
-    applied, factors = pl.pallas_call(
+    stacked, factors = pl.pallas_call(
         functools.partial(fields_kernel, n, planes, rows),
         out_shape=(
-            jax.ShapeDtypeStruct((slabs, 2 * w, nx), BF16),
-            jax.ShapeDtypeStruct((2, w, local_orbs), BF16),
+            jax.ShapeDtypeStruct((slabs, 3 * w, nx), BF16),
+            jax.ShapeDtypeStruct((3, w, local_orbs), BF16),
         ),
         in_specs=[vmem] * 7,
         out_specs=(vmem, vmem),
@@ -284,11 +319,10 @@
             collective_id=0, has_side_effects=True, vmem_limit_bytes=56 * 1024 * 1024
         ),
     )(
-        orb_r, adj_r, stored, gap_inverse, level_adj.reshape(w, 1),
-        window_cols.reshape(w, 1), potential.reshape(slabs, nx),
+        orb_r, adj_r, stored, gap_inverse, level_adj.reshape(1, w),
+        window_cols.reshape(1, w), potential.reshape(slabs, nx),
     )
-    stacked = jnp.concatenate([adj_r, applied], axis=1)
-    mix_t = jnp.concatenate([factors[0], factors[1], factors[0]], axis=0)
+    mix_t = factors.reshape(3 * w, local_orbs)
     result = lax.dot_general(
         mix_t, stacked, (((0,), (1,)), ((), ())), preferred_element_type=F32
     ).astype(BF16)

time: 121 us -> 105 us (0.87)
  Pallas kernels: 95.5 us -> 82.7 us
  local copies, waits for them, and re-layouts: 21 us -> 17.3 us
    pallas_call x1, Pallas kernels: 95.5 us -> 82.7 us  [local(): pl.pallas_call(functools.partial(fields_kernel, n, planes, rows), out_sha...]
    reshape x2 -> x0, local copies, waits for them, and re-layouts: 2.75 us -> none  [the longest x1 1.38 us: local(): level_adj.reshape(w, 1)]
    unnamed x6 -> x4, local copies, waits for them, and re-layouts: 10 us -> 10 us
where the time goes in v2:
time: 105 us
  Pallas kernels  82.7 us (79%)
  local copies, waits for them, and re-layouts  17.3 us (16%)
  matrix products  4.39 us (4%)
    pallas_call x1, Pallas kernels, local(): pl.pallas_call(functools.partial(fields_kernel, n, planes, rows), out_sha...  82.7 us
    unnamed x4, local copies, waits for them, and re-layouts  10 us
    reshape x1, local copies, waits for them, and re-layouts, local(): return result.reshape(orbitals.shape)  5.25 us
    dot_general x1, matrix products, local(): lax.dot_general(mix_t, stacked, (((0,), (1,)), ((), ())), preferred_eleme...  4.39 us

profile of v2, /device:TPU:0, one launch (start us, length us, event | category | flops | bytes accessed | tf_op | source)
XLA Modules:
  0.0 105.1 jit_solution(10151921011641823517)
XLA Ops:
  0.0 0.0 copy-start
  0.0 1.6 %copy-done = bf16[1024,1024]{1,0:T(8,128)(2,1)S(1)} copy-done((bf16[1024,1024]{1,0:T(8,128)(2,1)S(1)}, bf16[1024,1024]{1,0:T(8,128)(2,1)}, u32[]{:S(2)}) %copy-start) | copy-done | bytes 2097176
  1.6 0.7 pad_clamp_fusion
  2.3 2.6 %copy.10 = bf16[128,8,4,128]{3,0,2,1:T(8,128)(2,1)} copy(bf16[128,8,4,128]{3,2,1,0:T(4,128)(2,1)} %param.9) | data formatting | bytes 2097152 | tf_op args[1]
  4.9 2.0 %gather_fusion = bf16[8,128,1024]{2,1,0:T(8,128)(2,1)} fusion(bf16[8,128,1024]{2,1,0:T(8,128)(2,1)S(1)} %bitcast.17, s32[1024]{0:T(1024)S(1)} %pad_clamp_fusion), kind=kCustom, calls=%fused_computation | custom fusion | bytes 4194336 | tf_op jit(solution)/shard_map/jit(_take)/gather | solution.py:293
  6.9 5.8 %copy.9 = bf16[512,8,4,128]{3,0,2,1:T(8,128)(2,1)} copy(bf16[512,8,4,128]{3,2,1,0:T(4,128)(2,1)} %param.8) | data formatting | bytes 8388608 | tf_op args[0]
  12.8 82.7 %shard_map.82 = (bf16[32,384,128]{2,1,0:T(8,128)(2,1)}, bf16[3,128,512]{2,1,0:T(8,128)(2,1)}) custom-call(bf16[32,512,128]{2,1,0:T(8,128)(2,1)} %bitcast.18, bf16[32,128,128]{2,1,0:T(8,128)(2,1)} %bitcast.20, bf16[1024,1024]{1,0:T(8,128)(2,1)} %bitcast.19, f32[512,1024]{1,0:T(8,128)} %gap_ref.1, f32[1,128]{1,0:T(1,128)} %bitcast.23, s32[1,128]{1,0:T(1,128)} %bitcast.24, ...), custom_call_target="tpu_custom_call" | custom-call | tf_op jit(solution)/shard_map/pallas_call | solution.py:298
  95.4 4.4 %convolution_convert_fusion = bf16[512,32,128]{2,0,1:T(8,128)(2,1)S(1)} fusion(bf16[384,512,1]{1,0,2:T(8,128)(2,1)} %bitcast.25, bf16[32,384,128]{2,1,0:T(8,128)(2,1)} %get-tuple-element.8), kind=kOutput, calls=%fused_computation.1 | convolution fusion | flops 1612709888 | bytes 7733248 | tf_op jit(solution)/shard_map/dot_general | solution.py:326
  99.8 5.2 %copy.12 = bf16[512,8,4,128]{3,2,1,0:T(4,128)(2,1)} copy(bf16[512,8,4,128]{3,0,2,1:T(8,128)(2,1)S(1)} %bitcast.21) | data formatting | bytes 8388608 | tf_op jit(solution)/shard_map/reshape | solution.py:329
Async XLA Ops:
  0.0 1.6 %copy-start = (bf16[1024,1024]{1,0:T(8,128)(2,1)S(1)}, bf16[1024,1024]{1,0:T(8,128)(2,1)}, u32[]{:S(2)}) copy-start(bf16[1024,1024]{1,0:T(8,128)(2,1)} %param.11) | copy-start | bytes 6291460

commit v3 on v2

--- a/solution.py
+++ b/solution.py
@@ -31,8 +31,8 @@
 def fields_kernel(
     n, planes, rows,
     orb_ref, adj_ref, stored_ref, gap_ref, level_ref, cols_ref, pot_ref,
-    app_ref, fac_ref,
-    corr, rs_buf, ag_buf, gap_all, part, peer, wide,
+    out_ref,
+    app_ref, mix_ref, mixed_rows, corr, rs_buf, ag_buf, gap_all, part, peer, wide,
     rs_send, rs_recv, ag_send, ag_recv, gap_send, gap_recv,
     sum_send, sum_recv, up_send, up_recv, down_send, down_recv,
 ):
@@ -115,21 +115,36 @@
     hot = level_rows == column(cols_ref)
     hot16 = hot.astype(F32).astype(BF16)
     right_t = dot(hot16, stored_ref[mine, :], NT).astype(BF16)
-    fac_ref[0] = right_t
-    fac_ref[2] = right_t
+    mix_ref[:, :w] = right_t.astype(F32).T.astype(BF16)
+    mix_ref[:, 2 * w :] = mix_ref[:, :w]
 
     hi, mid, low = split3(gap_ref[...])
-    gap_all[o] = dot(hot16, hi, NT) + dot(hot16, mid, NT) + dot(hot16, low, NT)
-    gap_copy = pltpu.make_async_remote_copy(
-        src_ref=gap_all.at[o], dst_ref=gap_all.at[o],
-        send_sem=gap_send, recv_sem=gap_recv,
+    mine_gap = dot(hot16, hi, NT) + dot(hot16, mid, NT) + dot(hot16, low, NT)
+    gap_all[o] = mine_gap.reshape(n, w // n, local_orbs)
+    gap_cross = pltpu.make_async_remote_copy(
+        src_ref=gap_all.at[o, g], dst_ref=gap_all.at[o, g],
+        send_sem=gap_send.at[0], recv_sem=gap_recv.at[0],
         device_id=(g, other), device_id_type=MESH,
     )
+
+    def gap_copy(k):
+        return pltpu.make_async_remote_copy(
+            src_ref=gap_all.at[other, g], dst_ref=gap_all.at[other, g],
+            send_sem=gap_send.at[k], recv_sem=gap_recv.at[k],
+            device_id=(lax.rem(g + k, n), o), device_id_type=MESH,
+        )
+
+    def gap_start(k, _):
+        gap_copy(k).start()
+        return 0
+
     pl.semaphore_wait(barrier, n)
-    gap_copy.start()
+    gap_cross.start()
     partials(0, right_t)
     for ch in range(EARLY):
         sum_copy(0, ch).start()
+    gap_cross.wait_recv()
+    lax.fori_loop(1, n, gap_start, 0)
 
     corr[...] = jnp.zeros_like(corr)
 
@@ -182,6 +197,7 @@
     def ag_take(k, _):
         ag_copy(k, me, 0).wait_recv()
         ag_copy(k, theirs, n).wait_recv()
+        gap_copy(k).wait_recv()
         return 0
 
     cross_copy.start()
@@ -191,20 +207,19 @@
     cross_copy.wait_recv()
     lax.fori_loop(1, n, ag_forward, 0)
     lax.fori_loop(1, n, ag_take, 0)
-    gap_copy.wait_recv()
 
     corr_t = ag_buf[...].reshape(norb, w).T
     parts_t = jnp.concatenate(split3(corr_t), axis=0)
     rotated = dot(parts_t, stored_ref[...], NN)
     coupling_in = rotated[:w] + rotated[w : 2 * w] + rotated[2 * w :]
-    gap_cols = jnp.concatenate([gap_all[0], gap_all[1]], axis=1)
+    gap_cols = jnp.concatenate([gap_all[i].reshape(w, local_orbs) for i in range(2)], axis=1)
     coupling = gap_cols * coupling_in + jnp.where(hot, column(level_ref), 0.0)
     mixed = dot(jnp.concatenate(split3(coupling), axis=0), stored_ref[mine, :], NT)
     left_t = (mixed[:w] + mixed[w : 2 * w] + mixed[2 * w :]).astype(BF16)
-    fac_ref[1] = left_t
     partials(1, left_t)
     for ch in range(NCH):
         sum_copy(1, ch).start()
+    mix_ref[:, w : 2 * w] = left_t.astype(F32).T.astype(BF16)
 
     def combine(half, ch):
         i = half * NCH + ch
@@ -250,12 +265,27 @@
 
         lax.fori_loop(0, planes, step, 0)
 
+    def pair_of(k, fields):
+        return jnp.concatenate([app_ref[2 * k, fields], app_ref[2 * k + 1, fields]], axis=1)
+
+    def mix_first(k, _):
+        mixed_rows[k] = dot(mix_ref[:, : 2 * w], pair_of(k, slice(0, 2 * w)), NN)
+        return 0
+
+    def mix_last(k, _):
+        rest = dot(mix_ref[:, 2 * w :], pair_of(k, slice(2 * w, 3 * w)), NN)
+        value = (mixed_rows[k] + rest).astype(BF16)
+        out_ref[2 * k] = value[:, :nx]
+        out_ref[2 * k + 1] = value[:, nx:]
+        return 0
+
     for half in range(2):
         for ch in range(NCH):
             combine(half, ch)
             if ch:
                 stencil(half, ch - 1)
         stencil(half, NCH - 1)
+        lax.fori_loop(0, slabs // 2, (mix_first, mix_last)[half], 0)
 
     def rs_done(k, _):
         rs_copy(k).wait_send()
@@ -264,12 +294,13 @@
     def ag_done(k, _):
         ag_copy(k, me, 0).wait_send()
         ag_copy(k, theirs, n).wait_send()
+        gap_copy(k).wait_send()
         return 0
 
     lax.fori_loop(1, n, rs_done, 0)
     lax.fori_loop(1, n, ag_done, 0)
     cross_copy.wait_send()
-    gap_copy.wait_send()
+    gap_cross.wait_send()
     for half in range(2):
         for ch in range(NCH):
             sum_copy(half, ch).wait_send()
@@ -295,23 +326,23 @@
     ).reshape(norb, norb)
     vmem = pl.BlockSpec(memory_space=pltpu.VMEM)
     dma = pltpu.SemaphoreType.DMA
-    stacked, factors = pl.pallas_call(
+    result = pl.pallas_call(
         functools.partial(fields_kernel, n, planes, rows),
-        out_shape=(
-            jax.ShapeDtypeStruct((slabs, 3 * w, nx), BF16),
-            jax.ShapeDtypeStruct((3, w, local_orbs), BF16),
-        ),
+        out_shape=jax.ShapeDtypeStruct((slabs, local_orbs, nx), BF16),
         in_specs=[vmem] * 7,
-        out_specs=(vmem, vmem),
+        out_specs=vmem,
         scratch_shapes=[
+            pltpu.VMEM((slabs, 3 * w, nx), BF16),
+            pltpu.VMEM((local_orbs, 3 * w), BF16),
+            pltpu.VMEM((slabs // 2, local_orbs, 2 * nx), F32),
             pltpu.VMEM((n, chunk, w), F32),
             pltpu.VMEM((n, chunk, w), F32),
             pltpu.VMEM((2 * n, chunk, w), F32),
-            pltpu.VMEM((2, w, local_orbs), F32),
+            pltpu.VMEM((2, n, w // n, local_orbs), F32),
             pltpu.VMEM((2 * NCH, slabs, wc, nx), BF16),
             pltpu.VMEM((2 * NCH, slabs, wc, nx), BF16),
             pltpu.VMEM((2 * NCH, rows + 4, planes, wc, nx), BF16),
-            dma((n,)), dma((n,)), dma((2 * n,)), dma((2 * n,)), dma, dma,
+            dma((n,)), dma((n,)), dma((2 * n,)), dma((2 * n,)), dma((n,)), dma((n,)),
             dma((2 * NCH,)), dma((2 * NCH,)), dma((2 * NCH,)),
             dma((2 * NCH,)), dma((2 * NCH,)), dma((2 * NCH,)),
         ],
@@ -322,11 +353,7 @@
         orb_r, adj_r, stored, gap_inverse, level_adj.reshape(1, w),
         window_cols.reshape(1, w), potential.reshape(slabs, nx),
     )
-    mix_t = factors.reshape(3 * w, local_orbs)
-    result = lax.dot_general(
-        mix_t, stacked, (((0,), (1,)), ((), ())), preferred_element_type=F32
-    ).astype(BF16)
-    return result.reshape(orbitals.shape)
+    return result.transpose(1, 0, 2).reshape(orbitals.shape)
 
 
 def solution(mesh):

time: 105 us -> 115 us (1.095)
  Pallas kernels: 82.7 us -> 94.9 us
  matrix products: 4.39 us -> 0 us
  local copies, waits for them, and re-layouts: 17.3 us -> 19.5 us
    pallas_call x1, Pallas kernels: 82.7 us -> 94.9 us  [local(): pl.pallas_call(functools.partial(fields_kernel, n, planes, rows), out_sha...]
    dot_general x1 -> x0, matrix products: 4.39 us -> none  [local(): lax.dot_general(mix_t, stacked, (((0,), (1,)), ((), ())), preferred_eleme...]
    reshape x1, local copies, waits for them, and re-layouts: 5.25 us -> 7.44 us  [local(): return result.transpose(1, 0, 2).reshape(orbitals.shape)]
where the time goes in v3:
time: 115 us
  Pallas kernels  94.9 us (83%)
  local copies, waits for them, and re-layouts  19.5 us (17%)
    pallas_call x1, Pallas kernels, local(): pl.pallas_call(functools.partial(fields_kernel, n, planes, rows), out_sha...  94.9 us
    unnamed x4, local copies, waits for them, and re-layouts  10 us
    reshape x1, local copies, waits for them, and re-layouts, local(): return result.transpose(1, 0, 2).reshape(orbitals.shape)  7.44 us

profile of v3, /device:TPU:0, one launch (start us, length us, event | category | flops | bytes accessed | tf_op | source)
XLA Modules:
  0.0 115.0 jit_solution(8605292143161028952)
XLA Ops:
  0.0 0.0 copy-start
  0.0 1.6 %copy-done = bf16[1024,1024]{1,0:T(8,128)(2,1)S(1)} copy-done((bf16[1024,1024]{1,0:T(8,128)(2,1)S(1)}, bf16[1024,1024]{1,0:T(8,128)(2,1)}, u32[]{:S(2)}) %copy-start) | copy-done | bytes 2097176
  1.6 0.7 pad_clamp_fusion
  2.3 2.6 %copy.10 = bf16[128,8,4,128]{3,0,2,1:T(8,128)(2,1)} copy(bf16[128,8,4,128]{3,2,1,0:T(4,128)(2,1)} %param.9) | data formatting | bytes 2097152 | tf_op args[1]
  4.9 2.0 %gather_fusion = bf16[8,128,1024]{2,1,0:T(8,128)(2,1)} fusion(bf16[8,128,1024]{2,1,0:T(8,128)(2,1)S(1)} %bitcast.14, s32[1024]{0:T(1024)S(1)} %pad_clamp_fusion), kind=kCustom, calls=%fused_computation | custom fusion | bytes 4194336 | tf_op jit(solution)/shard_map/jit(_take)/gather | solution.py:324
  6.9 5.8 %copy.9 = bf16[512,8,4,128]{3,0,2,1:T(8,128)(2,1)} copy(bf16[512,8,4,128]{3,2,1,0:T(4,128)(2,1)} %param.8) | data formatting | bytes 8388608 | tf_op args[0]
  12.7 94.9 %shard_map.82 = bf16[32,512,128]{2,1,0:T(8,128)(2,1)} custom-call(bf16[32,512,128]{2,1,0:T(8,128)(2,1)} %bitcast.16, bf16[32,128,128]{2,1,0:T(8,128)(2,1)} %bitcast.18, bf16[1024,1024]{1,0:T(8,128)(2,1)} %bitcast.17, f32[512,1024]{1,0:T(8,128)} %gap_ref.1, f32[1,128]{1,0:T(1,128)} %bitcast.20, s32[1,128]{1,0:T(1,128)} %bitcast.21, f32[32,128]{1,0:T(8,128)} %bitcast.19), custom_call_target="tpu_custom_call" | custom-call | tf_op jit(solution)/shard_map/pallas_call | solution.py:329
  107.6 7.4 %copy.11 = bf16[512,8,4,128]{3,2,1,0:T(4,128)(2,1)} copy(bf16[512,8,4,128]{3,0,2,1:T(8,128)(2,1)} %bitcast.15) | data formatting | bytes 8388608 | tf_op jit(solution)/shard_map/reshape | solution.py:356
Async XLA Ops:
  0.0 1.6 %copy-start = (bf16[1024,1024]{1,0:T(8,128)(2,1)S(1)}, bf16[1024,1024]{1,0:T(8,128)(2,1)}, u32[]{:S(2)}) copy-start(bf16[1024,1024]{1,0:T(8,128)(2,1)} %param.11) | copy-start | bytes 6291460

commit v4 on v2

--- a/solution.py
+++ b/solution.py
@@ -8,8 +8,8 @@
 from jax.sharding import PartitionSpec as P
 
 MESH = pl.DeviceIdType.MESH
-NCH = 8
-EARLY = 2
+NCH = 4
+EARLY = 1
 F32 = jnp.float32
 BF16 = jnp.bfloat16
 NT = (((1,), (1,)), ((), ()))
@@ -18,6 +18,15 @@
 
 def dot(a, b, dims):
     return lax.dot_general(a, b, dims, preferred_element_type=F32)
+
+
+def loop(count, by, step):
+    def body(k, _):
+        for u in range(by):
+            step(k * by + u)
+        return 0
+
+    lax.fori_loop(0, count // by, body, 0)
 
 
 def split3(x):
@@ -95,7 +104,7 @@
         )
 
     def partials(half, factor_t):
-        def step(k, _):
+        def step(k):
             pair = jnp.concatenate([orb_ref[2 * k], orb_ref[2 * k + 1]], axis=1)
             term = dot(factor_t, pair, NN).astype(BF16)
             for ch in range(NCH):
@@ -104,7 +113,7 @@
                 part[half * NCH + ch, 2 * k + 1] = fields[:, nx:]
             return 0
 
-        lax.fori_loop(0, slabs // 2, step, 0)
+        loop(slabs // 2, 4, step)
 
     def column(row_ref):
         row = row_ref[...].astype(F32)
@@ -133,20 +142,20 @@
 
     corr[...] = jnp.zeros_like(corr)
 
-    def corr_step(k, _):
+    def corr_step(k):
         orbs = jnp.concatenate([orb_ref[4 * k + i] for i in range(4)], axis=1)
         adjs = jnp.concatenate([adj_ref[4 * k + i] for i in range(4)], axis=1)
         corr[...] += dot(orbs, adjs, NT).reshape(corr.shape)
         return 0
 
-    lax.fori_loop(0, slabs // 4, corr_step, 0)
+    loop(slabs // 4, 2, corr_step)
     lax.fori_loop(1, n, rs_start, 0)
 
-    def stack_step(r, _):
+    def stack_step(r):
         app_ref[r, :w] = adj_ref[r]
         return 0
 
-    lax.fori_loop(0, slabs, stack_step, 0)
+    loop(slabs, 4, stack_step)
 
     ag_buf[me] = corr[g]
 
@@ -210,7 +219,7 @@
         i = half * NCH + ch
         sum_copy(half, ch).wait_recv()
 
-        def step(p, _):
+        def step(p):
             for y in range(rows):
                 r = p * rows + y
                 wide[i, 2 + y, p] = (
@@ -218,7 +227,7 @@
                 ).astype(BF16)
             return 0
 
-        lax.fori_loop(0, planes, step, 0)
+        loop(planes, 4, step)
         up_copy(half, ch).start()
         down_copy(half, ch).start()
 
@@ -228,7 +237,7 @@
         down_copy(half, ch).wait_recv()
         first = (half + 1) * w + ch * wc
 
-        def step(p, _):
+        def step(p):
             lines = [wide[i, y, p].astype(F32) for y in range(rows + 4)]
             near_planes = [lax.rem(p + d, planes) for d in (1, planes - 1)]
             far_planes = [lax.rem(p + d, planes) for d in (2, planes - 2)]
@@ -248,7 +257,7 @@
                 app_ref[r, first : first + wc] = value.astype(BF16)
             return 0
 
-        lax.fori_loop(0, planes, step, 0)
+        loop(planes, 4, step)
 
     for half in range(2):
         for ch in range(NCH):

time: 105 us -> 93.9 us (0.89)
  Pallas kernels: 82.7 us -> 71.1 us
    pallas_call x1, Pallas kernels: 82.7 us -> 71.1 us  [local(): pl.pallas_call(functools.partial(fields_kernel, n, planes, rows), out_sha...]
where the time goes in v4:
time: 93.9 us; the launch traced here: 93.5 us
  Pallas kernels  71.1 us (76%)
  local copies, waits for them, and re-layouts  17.3 us (18%)
  matrix products  4.39 us (5%)
    pallas_call x1, Pallas kernels, local(): pl.pallas_call(functools.partial(fields_kernel, n, planes, rows), out_sha...  71.1 us
    unnamed x4, local copies, waits for them, and re-layouts  10 us
    reshape x1, local copies, waits for them, and re-layouts, local(): return result.reshape(orbitals.shape)  5.25 us
    dot_general x1, matrix products, local(): lax.dot_general(mix_t, stacked, (((0,), (1,)), ((), ())), preferred_eleme...  4.39 us
    gather x1, local copies, waits for them, and re-layouts, local(): jnp.take(rotation.reshape(tiles, norb // tiles, norb), tile_map, axis=0,...  2.04 us

profile of v4, /device:TPU:0, one launch (start us, length us, event | category | flops | bytes accessed | tf_op | source)
XLA Modules:
  0.0 93.5 jit_solution(5528229595100444467)
XLA Ops:
  0.0 0.0 copy-start
  0.0 1.6 %copy-done = bf16[1024,1024]{1,0:T(8,128)(2,1)S(1)} copy-done((bf16[1024,1024]{1,0:T(8,128)(2,1)S(1)}, bf16[1024,1024]{1,0:T(8,128)(2,1)}, u32[]{:S(2)}) %copy-start) | copy-done | bytes 2097176
  1.6 0.7 pad_clamp_fusion
  2.3 2.6 %copy.10 = bf16[128,8,4,128]{3,0,2,1:T(8,128)(2,1)} copy(bf16[128,8,4,128]{3,2,1,0:T(4,128)(2,1)} %param.9) | data formatting | bytes 2097152 | tf_op args[1]
  4.9 2.0 %gather_fusion = bf16[8,128,1024]{2,1,0:T(8,128)(2,1)} fusion(bf16[8,128,1024]{2,1,0:T(8,128)(2,1)S(1)} %bitcast.17, s32[1024]{0:T(1024)S(1)} %pad_clamp_fusion), kind=kCustom, calls=%fused_computation | custom fusion | bytes 4194336 | tf_op jit(solution)/shard_map/jit(_take)/gather | solution.py:302
  6.9 5.8 %copy.9 = bf16[512,8,4,128]{3,0,2,1:T(8,128)(2,1)} copy(bf16[512,8,4,128]{3,2,1,0:T(4,128)(2,1)} %param.8) | data formatting | bytes 8388608 | tf_op args[0]
  12.8 71.1 %shard_map.82 = (bf16[32,384,128]{2,1,0:T(8,128)(2,1)}, bf16[3,128,512]{2,1,0:T(8,128)(2,1)}) custom-call(bf16[32,512,128]{2,1,0:T(8,128)(2,1)} %bitcast.18, bf16[32,128,128]{2,1,0:T(8,128)(2,1)} %bitcast.20, bf16[1024,1024]{1,0:T(8,128)(2,1)} %bitcast.19, f32[512,1024]{1,0:T(8,128)} %gap_ref.1, f32[1,128]{1,0:T(1,128)} %bitcast.23, s32[1,128]{1,0:T(1,128)} %bitcast.24, ...), custom_call_target="tpu_custom_call" | custom-call | tf_op jit(solution)/shard_map/pallas_call | solution.py:307
  83.8 4.4 %convolution_convert_fusion = bf16[512,32,128]{2,0,1:T(8,128)(2,1)S(1)} fusion(bf16[384,512,1]{1,0,2:T(8,128)(2,1)} %bitcast.25, bf16[32,384,128]{2,1,0:T(8,128)(2,1)} %get-tuple-element.8), kind=kOutput, calls=%fused_computation.1 | convolution fusion | flops 1612709888 | bytes 7733248 | tf_op jit(solution)/shard_map/dot_general | solution.py:335
  88.2 5.2 %copy.12 = bf16[512,8,4,128]{3,2,1,0:T(4,128)(2,1)} copy(bf16[512,8,4,128]{3,0,2,1:T(8,128)(2,1)S(1)} %bitcast.21) | data formatting | bytes 8388608 | tf_op jit(solution)/shard_map/reshape | solution.py:338
Async XLA Ops:
  0.0 1.6 %copy-start = (bf16[1024,1024]{1,0:T(8,128)(2,1)S(1)}, bf16[1024,1024]{1,0:T(8,128)(2,1)}, u32[]{:S(2)}) copy-start(bf16[1024,1024]{1,0:T(8,128)(2,1)} %param.11) | copy-start | bytes 6291460

commit v5 on v4

--- a/solution.py
+++ b/solution.py
@@ -79,6 +79,18 @@
         rs_copy(k).start()
         return 0
 
+    corr[...] = jnp.zeros_like(corr)
+
+    def corr_step(k):
+        orbs = jnp.concatenate([orb_ref[4 * k + i] for i in range(4)], axis=1)
+        adjs = jnp.concatenate([adj_ref[4 * k + i] for i in range(4)], axis=1)
+        corr[...] += dot(orbs, adjs, NT).reshape(corr.shape)
+        return 0
+
+    loop(slabs // 4, 2, corr_step)
+    pl.semaphore_wait(barrier, n)
+    lax.fori_loop(1, n, rs_start, 0)
+
     def sum_copy(half, ch):
         i = half * NCH + ch
         return pltpu.make_async_remote_copy(
@@ -127,35 +139,31 @@
     fac_ref[0] = right_t
     fac_ref[2] = right_t
 
-    hi, mid, low = split3(gap_ref[...])
-    gap_all[o] = dot(hot16, hi, NT) + dot(hot16, mid, NT) + dot(hot16, low, NT)
-    gap_copy = pltpu.make_async_remote_copy(
-        src_ref=gap_all.at[o], dst_ref=gap_all.at[o],
-        send_sem=gap_send, recv_sem=gap_recv,
-        device_id=(g, other), device_id_type=MESH,
-    )
-    pl.semaphore_wait(barrier, n)
-    gap_copy.start()
     partials(0, right_t)
     for ch in range(EARLY):
         sum_copy(0, ch).start()
 
-    corr[...] = jnp.zeros_like(corr)
-
-    def corr_step(k):
-        orbs = jnp.concatenate([orb_ref[4 * k + i] for i in range(4)], axis=1)
-        adjs = jnp.concatenate([adj_ref[4 * k + i] for i in range(4)], axis=1)
-        corr[...] += dot(orbs, adjs, NT).reshape(corr.shape)
-        return 0
-
-    loop(slabs // 4, 2, corr_step)
-    lax.fori_loop(1, n, rs_start, 0)
-
-    def stack_step(r):
-        app_ref[r, :w] = adj_ref[r]
-        return 0
-
-    loop(slabs, 4, stack_step)
+    hi, mid, low = split3(gap_ref[...])
+    mine_gap = dot(hot16, hi, NT) + dot(hot16, mid, NT) + dot(hot16, low, NT)
+    gap_all[o] = mine_gap.reshape(n, w // n, local_orbs)
+    gap_cross = pltpu.make_async_remote_copy(
+        src_ref=gap_all.at[o, g], dst_ref=gap_all.at[o, g],
+        send_sem=gap_send.at[0], recv_sem=gap_recv.at[0],
+        device_id=(g, other), device_id_type=MESH,
+    )
+
+    def gap_copy(k):
+        return pltpu.make_async_remote_copy(
+            src_ref=gap_all.at[other, g], dst_ref=gap_all.at[other, g],
+            send_sem=gap_send.at[k], recv_sem=gap_recv.at[k],
+            device_id=(lax.rem(g + k, n), o), device_id_type=MESH,
+        )
+
+    def gap_start(k, _):
+        gap_copy(k).start()
+        return 0
+
+    gap_cross.start()
 
     ag_buf[me] = corr[g]
 
@@ -191,6 +199,7 @@
     def ag_take(k, _):
         ag_copy(k, me, 0).wait_recv()
         ag_copy(k, theirs, n).wait_recv()
+        gap_copy(k).wait_recv()
         return 0
 
     cross_copy.start()
@@ -199,14 +208,15 @@
         sum_copy(0, ch).start()
     cross_copy.wait_recv()
     lax.fori_loop(1, n, ag_forward, 0)
+    gap_cross.wait_recv()
+    lax.fori_loop(1, n, gap_start, 0)
     lax.fori_loop(1, n, ag_take, 0)
-    gap_copy.wait_recv()
 
     corr_t = ag_buf[...].reshape(norb, w).T
     parts_t = jnp.concatenate(split3(corr_t), axis=0)
     rotated = dot(parts_t, stored_ref[...], NN)
     coupling_in = rotated[:w] + rotated[w : 2 * w] + rotated[2 * w :]
-    gap_cols = jnp.concatenate([gap_all[0], gap_all[1]], axis=1)
+    gap_cols = jnp.concatenate([gap_all[i].reshape(w, local_orbs) for i in range(2)], axis=1)
     coupling = gap_cols * coupling_in + jnp.where(hot, column(level_ref), 0.0)
     mixed = dot(jnp.concatenate(split3(coupling), axis=0), stored_ref[mine, :], NT)
     left_t = (mixed[:w] + mixed[w : 2 * w] + mixed[2 * w :]).astype(BF16)
@@ -214,6 +224,12 @@
     partials(1, left_t)
     for ch in range(NCH):
         sum_copy(1, ch).start()
+
+    def stack_step(r):
+        app_ref[r, :w] = adj_ref[r]
+        return 0
+
+    loop(slabs, 4, stack_step)
 
     def combine(half, ch):
         i = half * NCH + ch
@@ -273,12 +289,13 @@
     def ag_done(k, _):
         ag_copy(k, me, 0).wait_send()
         ag_copy(k, theirs, n).wait_send()
+        gap_copy(k).wait_send()
         return 0
 
     lax.fori_loop(1, n, rs_done, 0)
     lax.fori_loop(1, n, ag_done, 0)
     cross_copy.wait_send()
-    gap_copy.wait_send()
+    gap_cross.wait_send()
     for half in range(2):
         for ch in range(NCH):
             sum_copy(half, ch).wait_send()
@@ -316,11 +333,11 @@
             pltpu.VMEM((n, chunk, w), F32),
             pltpu.VMEM((n, chunk, w), F32),
             pltpu.VMEM((2 * n, chunk, w), F32),
-            pltpu.VMEM((2, w, local_orbs), F32),
+            pltpu.VMEM((2, n, w // n, local_orbs), F32),
             pltpu.VMEM((2 * NCH, slabs, wc, nx), BF16),
             pltpu.VMEM((2 * NCH, slabs, wc, nx), BF16),
             pltpu.VMEM((2 * NCH, rows + 4, planes, wc, nx), BF16),
-            dma((n,)), dma((n,)), dma((2 * n,)), dma((2 * n,)), dma, dma,
+            dma((n,)), dma((n,)), dma((2 * n,)), dma((2 * n,)), dma((n,)), dma((n,)),
             dma((2 * NCH,)), dma((2 * NCH,)), dma((2 * NCH,)),
             dma((2 * NCH,)), dma((2 * NCH,)), dma((2 * NCH,)),
         ],

time: 93.9 us -> 94.5 us (level)
  no operation moved by 1% of the time
where the time goes in v5:
time: 94.5 us; the launch traced here: 94.2 us
  Pallas kernels  71.8 us (76%)
  local copies, waits for them, and re-layouts  17.3 us (18%)
  matrix products  4.39 us (5%)
    pallas_call x1, Pallas kernels, local(): pl.pallas_call(functools.partial(fields_kernel, n, planes, rows), out_sha...  71.8 us
    unnamed x4, local copies, waits for them, and re-layouts  10 us
    reshape x1, local copies, waits for them, and re-layouts, local(): return result.reshape(orbitals.shape)  5.25 us
    dot_general x1, matrix products, local(): lax.dot_general(mix_t, stacked, (((0,), (1,)), ((), ())), preferred_eleme...  4.39 us
    gather x1, local copies, waits for them, and re-layouts, local(): jnp.take(rotation.reshape(tiles, norb // tiles, norb), tile_map, axis=0,...  2.04 us

profile of v5, /device:TPU:0, one launch (start us, length us, event | category | flops | bytes accessed | tf_op | source)
XLA Modules:
  0.0 94.2 jit_solution(14316873494170558337)
XLA Ops:
  0.0 0.0 copy-start
  0.0 1.6 %copy-done = bf16[1024,1024]{1,0:T(8,128)(2,1)S(1)} copy-done((bf16[1024,1024]{1,0:T(8,128)(2,1)S(1)}, bf16[1024,1024]{1,0:T(8,128)(2,1)}, u32[]{:S(2)}) %copy-start) | copy-done | bytes 2097176
  1.6 0.7 pad_clamp_fusion
  2.3 2.6 %copy.10 = bf16[128,8,4,128]{3,0,2,1:T(8,128)(2,1)} copy(bf16[128,8,4,128]{3,2,1,0:T(4,128)(2,1)} %param.9) | data formatting | bytes 2097152 | tf_op args[1]
  4.9 2.0 %gather_fusion = bf16[8,128,1024]{2,1,0:T(8,128)(2,1)} fusion(bf16[8,128,1024]{2,1,0:T(8,128)(2,1)S(1)} %bitcast.17, s32[1024]{0:T(1024)S(1)} %pad_clamp_fusion), kind=kCustom, calls=%fused_computation | custom fusion | bytes 4194336 | tf_op jit(solution)/shard_map/jit(_take)/gather | solution.py:319
  6.9 5.8 %copy.9 = bf16[512,8,4,128]{3,0,2,1:T(8,128)(2,1)} copy(bf16[512,8,4,128]{3,2,1,0:T(4,128)(2,1)} %param.8) | data formatting | bytes 8388608 | tf_op args[0]
  12.8 71.8 %shard_map.82 = (bf16[32,384,128]{2,1,0:T(8,128)(2,1)}, bf16[3,128,512]{2,1,0:T(8,128)(2,1)}) custom-call(bf16[32,512,128]{2,1,0:T(8,128)(2,1)} %bitcast.18, bf16[32,128,128]{2,1,0:T(8,128)(2,1)} %bitcast.20, bf16[1024,1024]{1,0:T(8,128)(2,1)} %bitcast.19, f32[512,1024]{1,0:T(8,128)} %gap_ref.1, f32[1,128]{1,0:T(1,128)} %bitcast.23, s32[1,128]{1,0:T(1,128)} %bitcast.24, ...), custom_call_target="tpu_custom_call" | custom-call | tf_op jit(solution)/shard_map/pallas_call | solution.py:324
  84.6 4.4 %convolution_convert_fusion = bf16[512,32,128]{2,0,1:T(8,128)(2,1)S(1)} fusion(bf16[384,512,1]{1,0,2:T(8,128)(2,1)} %bitcast.25, bf16[32,384,128]{2,1,0:T(8,128)(2,1)} %get-tuple-element.8), kind=kOutput, calls=%fused_computation.1 | convolution fusion | flops 1612709888 | bytes 7733248 | tf_op jit(solution)/shard_map/dot_general | solution.py:352
  89.0 5.2 %copy.12 = bf16[512,8,4,128]{3,2,1,0:T(4,128)(2,1)} copy(bf16[512,8,4,128]{3,0,2,1:T(8,128)(2,1)S(1)} %bitcast.21) | data formatting | bytes 8388608 | tf_op jit(solution)/shard_map/reshape | solution.py:355
Async XLA Ops:
  0.0 1.6 %copy-start = (bf16[1024,1024]{1,0:T(8,128)(2,1)S(1)}, bf16[1024,1024]{1,0:T(8,128)(2,1)}, u32[]{:S(2)}) copy-start(bf16[1024,1024]{1,0:T(8,128)(2,1)} %param.11) | copy-start | bytes 6291460

commit v6 on v5

--- a/solution.py
+++ b/solution.py
@@ -87,7 +87,7 @@
         corr[...] += dot(orbs, adjs, NT).reshape(corr.shape)
         return 0
 
-    loop(slabs // 4, 2, corr_step)
+    loop(slabs // 4, 4, corr_step)
     pl.semaphore_wait(barrier, n)
     lax.fori_loop(1, n, rs_start, 0)
 
@@ -125,7 +125,7 @@
                 part[half * NCH + ch, 2 * k + 1] = fields[:, nx:]
             return 0
 
-        loop(slabs // 2, 4, step)
+        loop(slabs // 2, 8, step)
 
     def column(row_ref):
         row = row_ref[...].astype(F32)
@@ -243,7 +243,7 @@
                 ).astype(BF16)
             return 0
 
-        loop(planes, 4, step)
+        loop(planes, planes, step)
         up_copy(half, ch).start()
         down_copy(half, ch).start()
 
@@ -273,7 +273,7 @@
                 app_ref[r, first : first + wc] = value.astype(BF16)
             return 0
 
-        loop(planes, 4, step)
+        loop(planes, planes, step)
 
     for half in range(2):
         for ch in range(NCH):

time: 94.5 us -> 94.2 us (level)
  no operation moved by 1% of the time
where the time goes in v6:
time: 94.2 us; the launch traced here: 94 us
  Pallas kernels  71.6 us (76%)
  local copies, waits for them, and re-layouts  17.3 us (18%)
  matrix products  4.39 us (5%)
    pallas_call x1, Pallas kernels, local(): pl.pallas_call(functools.partial(fields_kernel, n, planes, rows), out_sha...  71.6 us
    unnamed x4, local copies, waits for them, and re-layouts  10 us
    reshape x1, local copies, waits for them, and re-layouts, local(): return result.reshape(orbitals.shape)  5.25 us
    dot_general x1, matrix products, local(): lax.dot_general(mix_t, stacked, (((0,), (1,)), ((), ())), preferred_eleme...  4.39 us
    gather x1, local copies, waits for them, and re-layouts, local(): jnp.take(rotation.reshape(tiles, norb // tiles, norb), tile_map, axis=0,...  2.04 us

profile of v6, /device:TPU:0, one launch (start us, length us, event | category | flops | bytes accessed | tf_op | source)
XLA Modules:
  0.0 94.0 jit_solution(3955181986434387571)
XLA Ops:
  0.0 0.0 copy-start
  0.0 1.6 %copy-done = bf16[1024,1024]{1,0:T(8,128)(2,1)S(1)} copy-done((bf16[1024,1024]{1,0:T(8,128)(2,1)S(1)}, bf16[1024,1024]{1,0:T(8,128)(2,1)}, u32[]{:S(2)}) %copy-start) | copy-done | bytes 2097176
  1.6 0.7 pad_clamp_fusion
  2.3 2.6 %copy.10 = bf16[128,8,4,128]{3,0,2,1:T(8,128)(2,1)} copy(bf16[128,8,4,128]{3,2,1,0:T(4,128)(2,1)} %param.9) | data formatting | bytes 2097152 | tf_op args[1]
  4.9 2.0 %gather_fusion = bf16[8,128,1024]{2,1,0:T(8,128)(2,1)} fusion(bf16[8,128,1024]{2,1,0:T(8,128)(2,1)S(1)} %bitcast.17, s32[1024]{0:T(1024)S(1)} %pad_clamp_fusion), kind=kCustom, calls=%fused_computation | custom fusion | bytes 4194336 | tf_op jit(solution)/shard_map/jit(_take)/gather | solution.py:319
  6.9 5.8 %copy.9 = bf16[512,8,4,128]{3,0,2,1:T(8,128)(2,1)} copy(bf16[512,8,4,128]{3,2,1,0:T(4,128)(2,1)} %param.8) | data formatting | bytes 8388608 | tf_op args[0]
  12.8 71.6 %shard_map.82 = (bf16[32,384,128]{2,1,0:T(8,128)(2,1)}, bf16[3,128,512]{2,1,0:T(8,128)(2,1)}) custom-call(bf16[32,512,128]{2,1,0:T(8,128)(2,1)} %bitcast.18, bf16[32,128,128]{2,1,0:T(8,128)(2,1)} %bitcast.20, bf16[1024,1024]{1,0:T(8,128)(2,1)} %bitcast.19, f32[512,1024]{1,0:T(8,128)} %gap_ref.1, f32[1,128]{1,0:T(1,128)} %bitcast.23, s32[1,128]{1,0:T(1,128)} %bitcast.24, ...), custom_call_target="tpu_custom_call" | custom-call | tf_op jit(solution)/shard_map/pallas_call | solution.py:324
  84.3 4.4 %convolution_convert_fusion = bf16[512,32,128]{2,0,1:T(8,128)(2,1)S(1)} fusion(bf16[384,512,1]{1,0,2:T(8,128)(2,1)} %bitcast.25, bf16[32,384,128]{2,1,0:T(8,128)(2,1)} %get-tuple-element.8), kind=kOutput, calls=%fused_computation.1 | convolution fusion | flops 1612709888 | bytes 7733248 | tf_op jit(solution)/shard_map/dot_general | solution.py:352
  88.7 5.2 %copy.12 = bf16[512,8,4,128]{3,2,1,0:T(4,128)(2,1)} copy(bf16[512,8,4,128]{3,0,2,1:T(8,128)(2,1)S(1)} %bitcast.21) | data formatting | bytes 8388608 | tf_op jit(solution)/shard_map/reshape | solution.py:355
Async XLA Ops:
  0.0 1.6 %copy-start = (bf16[1024,1024]{1,0:T(8,128)(2,1)S(1)}, bf16[1024,1024]{1,0:T(8,128)(2,1)}, u32[]{:S(2)}) copy-start(bf16[1024,1024]{1,0:T(8,128)(2,1)} %param.11) | copy-start | bytes 6291460
